TPU v7x, 512 devices: a whole 4x8x8 slice. The times are simulated.
512 devices in a mesh: traj: 32 (over x, y), cand: 16 (over z, core).
Axes of the slice: x: 4, y: 8, z: 8, core: 2. Of those that a mesh axis runs over, the one named last changes fastest.
Arguments:
- state: float32 [4096, 256], P('traj'), may hold values from -6 to 6
- target: float32 [4096, 256], P('traj'), may hold values from -6 to 6
- coeffs: bfloat16 [33280, 256], P('cand'), may hold values from -6 to 6
- pairs: int32 [2, 33280], P(None, 'cand'), may hold values from 0 to 256, as said below
- mask: int32 [33280, 256], P('cand'), may hold values 0 or 1
Outputs:
- slope: float32 [4096, 256], P('traj')
- new_coeffs: bfloat16 [33280, 256], P('cand')
Inputs may be any that keep to these rules, and one draw needn't show every extreme that they name: Each column holds a pair pairs[0, c] <= pairs[1, c]; index 256 stands for the constant 1; no pair repeats before every pair has appeared.
All inputs are finite; a program needn't handle non-finite values. No bound on the sum of `mask` on one device may be relied on, other than what follows from the above.
Results may differ from a plain program's by a relative error of at most 0.014.
Values may be sent and summed in bfloat16 or wider, within the bound.
No kernel may reach another device: no remote copies, remote signals or barrier semaphores. Data moves between devices by JAX's collectives and lax.ppermute only.
A program may use at most 64 MiB of HBM per device.

v0:
```python
import math
import jax
import jax.numpy as jnp
from jax import lax
from jax.sharding import PartitionSpec as P

CANDS = 33280
step_dt = 0.25


def body(state, target, coeffs, pairs, mask):
    rows, modes_count = state.shape
    left = pairs[0]
    right = pairs[1]
    scale = 1.0 / math.sqrt(CANDS)
    segments = rows * lax.axis_size("traj")
    modes = jnp.arange(modes_count, dtype=jnp.int32)
    jac_left = (left[:, None] == modes[None, :]).astype(jnp.bfloat16)
    jac_right = (right[:, None] == modes[None, :]).astype(jnp.bfloat16)
    ones_col = jnp.ones((rows, 1), jnp.float32)

    def factors(y):
        z = jnp.concatenate([y, ones_col], 1)
        return (jnp.take(z, left, axis=1), jnp.take(z, right, axis=1))

    def library(y):
        left_vals, right_vals = factors(y)
        return (left_vals * right_vals).astype(jnp.bfloat16)

    def derive(theta):
        partial_rate = jnp.dot(theta, coeffs, preferred_element_type=jnp.float32) * scale
        return lax.psum(partial_rate, "cand")

    def pullback(cot, y):
        hidden = (
            lax.dot_general(
                cot.astype(jnp.bfloat16),
                coeffs,
                (((1,), (1,)), ((), ())),
                preferred_element_type=jnp.float32,
            )
            * scale
        )
        left_vals, right_vals = factors(y)
        upper = (hidden * right_vals).astype(jnp.bfloat16)
        lower = (hidden * left_vals).astype(jnp.bfloat16)
        partial_cot = jnp.dot(upper, jac_left, preferred_element_type=jnp.float32)
        partial_cot = partial_cot + jnp.dot(lower, jac_right, preferred_element_type=jnp.float32)
        return lax.psum(partial_cot, "cand")

    y_two = None
    th1 = library(state)
    k1 = derive(th1)
    y_two = state + 0.5 * step_dt * k1
    th2 = library(y_two)
    k2 = derive(th2)
    y_three = state + 0.5 * step_dt * k2
    th3 = library(y_three)
    k3 = derive(th3)
    y_four = state + step_dt * k3
    th4 = library(y_four)
    k4 = derive(th4)
    slope = (k1 + 2.0 * k2 + 2.0 * k3 + k4) / 6.0
    cot = (state + step_dt * slope - target) / segments
    g4 = step_dt / 6.0 * cot
    c4 = pullback(g4, y_four)
    g3 = step_dt / 3.0 * cot + step_dt * c4
    c3 = pullback(g3, y_three)
    g2 = step_dt / 3.0 * cot + 0.5 * step_dt * c3
    c2 = pullback(g2, y_two)
    g1 = step_dt / 6.0 * cot + 0.5 * step_dt * c2

    def outer(theta, grad_cot):
        return lax.dot_general(
            theta,
            grad_cot.astype(jnp.bfloat16),
            (((0,), (0,)), ((), ())),
            preferred_element_type=jnp.float32,
        )

    grad = (outer(th1, g1) + outer(th2, g2) + outer(th3, g3) + outer(th4, g4)) * scale
    rate = 0.5 * math.sqrt(segments * CANDS) / step_dt
    total = lax.psum(grad, "traj")
    fresh = (mask.astype(jnp.float32) * (coeffs.astype(jnp.float32) - rate * total)).astype(
        jnp.bfloat16
    )
    return (slope, fresh)


def solution(mesh):
    placed = (P("traj", None), P("traj", None), P("cand", None), P(None, "cand"), P("cand", None))
    return jax.shard_map(
        body,
        mesh=mesh,
        in_specs=placed,
        out_specs=(P("traj", None), P("cand", None)),
        check_vma=False,
    )
```

profile of v0, /device:TPU:16, one launch (start us, length us, event | category | flops | bytes accessed | tf_op | source)
XLA Modules:
  0.0 1064.3 jit_solution(13873290852304407379)
XLA Ops:
  9.1 3.9 gather_fusion.1
  13.1 5.1 gather_fusion
  18.2 3.0 fusion.19
  21.2 1.0 convolution_multiply_fusion.6
  22.2 118.2 %all-reduce.13.cloned.1.call-done = f32[128,256]{1,0:T(8,128)} async-done(((f32[128,256]{1,0:T(8,128)}), f32[128,256]{1,0:T(8,128)}) %all-reduce.13.cloned.1.call-update) | async-done | bytes 131088 | tf_op jit(solution)/shard_map/psum | solution.py:32
  141.5 3.9 gather_fusion.3
  145.4 3.9 gather_fusion.2
  149.4 1.4 fusion.16
  151.6 1.0 convolution_multiply_fusion.5
  152.7 113.5 %all-reduce.15.cloned.1.call-done = f32[128,256]{1,0:T(8,128)} async-done(((f32[128,256]{1,0:T(8,128)}), f32[128,256]{1,0:T(8,128)}) %all-reduce.15.cloned.1.call-update) | async-done | bytes 131088 | tf_op jit(solution)/shard_map/psum | solution.py:32
  268.8 5.1 gather_fusion.5
  273.9 5.0 gather_fusion.4
  278.9 3.1 fusion.13
  282.8 1.0 convolution_multiply_fusion.4
  283.9 113.5 %all-reduce.17.cloned.1.call-done = f32[128,256]{1,0:T(8,128)} async-done(((f32[128,256]{1,0:T(8,128)}), f32[128,256]{1,0:T(8,128)}) %all-reduce.17.cloned.1.call-update) | async-done | bytes 131088 | tf_op jit(solution)/shard_map/psum | solution.py:32
  400.0 5.1 gather_fusion.7
  405.1 5.0 gather_fusion.6
  410.1 3.1 fusion.10
  414.0 1.0 convolution_multiply_fusion.3
  415.1 113.5 %all-reduce.19.cloned.1.call-done = f32[128,256]{1,0:T(8,128)} async-done(((f32[128,256]{1,0:T(8,128)}), f32[128,256]{1,0:T(8,128)}) %all-reduce.19.cloned.1.call-update) | async-done | bytes 131088 | tf_op jit(solution)/shard_map/psum | solution.py:32
  528.6 1.9 add_subtract_fusion
  532.9 1.7 fusion.7
  534.7 113.5 %all-reduce.21.cloned.1.call-done = f32[128,256]{1,0:T(8,128)} async-done(((f32[128,256]{1,0:T(8,128)}), f32[128,256]{1,0:T(8,128)}) %all-reduce.21.cloned.1.call-update) | async-done | bytes 131088 | tf_op jit(solution)/shard_map/psum | solution.py:49
  651.6 1.7 fusion.8
  653.5 113.3 %all-reduce.23.cloned.1.call-done = f32[128,256]{1,0:T(8,128)} async-done(((f32[128,256]{1,0:T(8,128)}), f32[128,256]{1,0:T(8,128)}) %all-reduce.23.cloned.1.call-update) | async-done | bytes 131088 | tf_op jit(solution)/shard_map/psum | solution.py:49
  769.2 1.7 fusion.9
  771.0 113.5 %all-reduce.25.cloned.1.call-done = f32[128,256]{1,0:T(8,128)} async-done(((f32[128,256]{1,0:T(8,128)}), f32[128,256]{1,0:T(8,128)}) %all-reduce.25.cloned.1.call-update) | async-done | bytes 131088 | tf_op jit(solution)/shard_map/psum | solution.py:49
  884.5 1.3 fusion.44
  885.8 1.5 convolution_add_fusion.2
  888.4 1.8 fusion
  890.9 163.6 %all-reduce.27.cloned.1.call-done = f32[2080,256]{1,0:T(8,128)} async-done(((f32[2080,256]{1,0:T(8,128)}), f32[2080,256]{1,0:T(8,128)}) %all-reduce.27.cloned.1.call-update) | async-done | bytes 2129936 | tf_op jit(solution)/shard_map/psum | solution.py:83
  1054.5 3.0 multiply_convert_fusion
  (72 shorter events, 21.0 us)
Async XLA Ops:
  7.2 133.3 %all-reduce.13.cloned.1.call-start = ((), (), s32[]{:S(2)}) async-start(), calls=%async_computation | async-start | bytes 262144 | tf_op jit(solution)/shard_map/psum | solution.py:32
  18.1 3.0 copy-start
  21.1 120.2 %copy-start.10 = (bf16[128,2080]{0,1:T(8,128)(2,1)}, bf16[128,2080]{0,1:T(8,128)(2,1)S(1)}, u32[]{:S(2)}) copy-start(bf16[128,2080]{0,1:T(8,128)(2,1)S(1)} %fusion.19) | copy-start | bytes 1597444
  21.1 119.3 %copy-start.12 = (f32[128,256]{1,0:T(8,128)S(1)}, f32[128,256]{1,0:T(8,128)}, u32[]{:S(2)}) copy-start(f32[128,256]{1,0:T(8,128)} %param.7) | copy-start | bytes 393220
  22.2 244.0 %all-reduce.15.cloned.1.call-start = ((), (), s32[]{:S(2)}) async-start(), calls=%async_computation.1 | async-start | bytes 262144 | tf_op jit(solution)/shard_map/psum | solution.py:32
  150.8 0.8 copy-start.5
  152.6 244.8 %all-reduce.17.cloned.1.call-start = ((), (), s32[]{:S(2)}) async-start(), calls=%async_computation.2 | async-start | bytes 262144 | tf_op jit(solution)/shard_map/psum | solution.py:32
  282.0 0.8 copy-start.6
  283.8 244.8 %all-reduce.19.cloned.1.call-start = ((), (), s32[]{:S(2)}) async-start(), calls=%async_computation.3 | async-start | bytes 262144 | tf_op jit(solution)/shard_map/psum | solution.py:32
  413.2 0.8 copy-start.8
  415.0 233.2 %all-reduce.21.cloned.1.call-start = ((), (), s32[]{:S(2)}) async-start(), calls=%async_computation.4 | async-start | bytes 262144 | tf_op jit(solution)/shard_map/psum | solution.py:49
  530.5 1.2 copy-start.4
  531.7 1.2 copy-start.3
  534.6 232.2 %all-reduce.23.cloned.1.call-start = ((), (), s32[]{:S(2)}) async-start(), calls=%async_computation.5 | async-start | bytes 262144 | tf_op jit(solution)/shard_map/psum | solution.py:49
  649.1 1.2 copy-start.2
  650.4 1.2 copy-start.1
  653.3 231.2 %all-reduce.25.cloned.1.call-start = ((), (), s32[]{:S(2)}) async-start(), calls=%async_computation.6 | async-start | bytes 262144 | tf_op jit(solution)/shard_map/psum | solution.py:49
  769.2 115.3 %copy-start.11 = (bf16[128,2080]{0,1:T(8,128)(2,1)S(1)}, bf16[128,2080]{0,1:T(8,128)(2,1)}, u32[]{:S(2)}) copy-start(bf16[128,2080]{0,1:T(8,128)(2,1)} %copy-done.10) | copy-start | bytes 1597444
  770.9 283.5 %all-reduce.27.cloned.1.call-start = ((), (), s32[]{:S(2)}) async-start(), calls=%async_computation.7 | async-start | bytes 4259840 | tf_op jit(solution)/shard_map/psum | solution.py:83
  885.8 1.5 copy-start.7
  887.4 1.0 copy-start.9
  888.4 1.8 copy-start.14
  890.2 164.3 %copy-start.13 = (s32[2080,256]{1,0:T(8,128)S(1)}, s32[2080,256]{1,0:T(8,128)}, u32[]{:S(2)}) copy-start(s32[2080,256]{1,0:T(8,128)} %param.11) | copy-start | bytes 6389764
Sparse Core Ops, SparseCore 0:
  22.3 118.0 all-reduce.12
  152.7 113.4 all-reduce.14
  284.0 113.4 all-reduce.16
  415.2 113.4 all-reduce.18
  534.8 113.4 all-reduce.20
  653.4 113.4 all-reduce.22
  771.0 113.3 all-reduce.24
  890.3 164.0 all-reduce.26
where the time goes:
time: 1060 us
  waiting for transfers between devices  963 us (91%)
  local copies, waits for them, and re-layouts  47.4 us (4%)
  other arithmetic  20.6 us (2%)
  matrix products  18.4 us (2%)
  between operations  14.5 us (1%)
    psum x4, waiting for transfers between devices, derive(): return lax.psum(partial_rate, 'cand')  459 us
    psum x3, waiting for transfers between devices, pullback(): return lax.psum(partial_cot, 'cand')  340 us
    psum x1, waiting for transfers between devices, body(): total = lax.psum(grad, 'traj')  164 us
    gather x8, local copies, waits for them, and re-layouts, factors(): return (jnp.take(z, left, axis=1), jnp.take(z, right, axis=1))  37.1 us
  transfers between devices with their start and end apart: 8, of which 8 were waited for; matrix products, arithmetic and copies ran while one was open for 0% of the time, Pallas kernels for 0%

commit v1 on v0

--- a/solution.py
+++ b/solution.py
@@ -29,7 +29,11 @@
 
     def derive(theta):
         partial_rate = jnp.dot(theta, coeffs, preferred_element_type=jnp.float32) * scale
-        return lax.psum(partial_rate, "cand")
+
+        def _store_threads(here_x):
+            return jnp.sum(jax.lax.all_gather(here_x, "cand"), 0)
+
+        return _store_threads(partial_rate)
 
     def pullback(cot, y):
         hidden = (

time: 1060 us -> 785 us (0.74)
  waiting for transfers between devices: 963 us -> 674 us
    psum x4 -> x0, waiting for transfers between devices: 459 us -> none  [derive(): return lax.psum(partial_rate, 'cand')]
    all_gather x0 -> x4, waiting for transfers between devices: none -> 172 us  [_store_threads(): return jnp.sum(jax.lax.all_gather(here_x, 'cand'), 0)]
where the time goes in v1:
time: 785 us; the launch traced here: 784 us
  waiting for transfers between devices  674 us (86%)
  local copies, waits for them, and re-layouts  49.9 us (6%)
  other arithmetic  26.9 us (3%)
  matrix products  18.3 us (2%)
  between operations  14.5 us (2%)
    psum x3, waiting for transfers between devices, pullback(): return lax.psum(partial_cot, 'cand')  339 us
    all_gather x4, waiting for transfers between devices, _store_threads(): return jnp.sum(jax.lax.all_gather(here_x, 'cand'), 0)  172 us
    psum x1, waiting for transfers between devices, body(): total = lax.psum(grad, 'traj')  164 us
    gather x8, local copies, waits for them, and re-layouts, factors(): return (jnp.take(z, left, axis=1), jnp.take(z, right, axis=1))  37.1 us
  transfers between devices with their start and end apart: 8, of which 8 were waited for; matrix products, arithmetic and copies ran while one was open for 0% of the time, Pallas kernels for 0%

profile of v1, /device:TPU:16, one launch (start us, length us, event | category | flops | bytes accessed | tf_op | source)
XLA Modules:
  0.0 784.3 jit_solution(2606318454699575099)
XLA Ops:
  9.1 3.9 gather_fusion.1
  13.1 5.1 gather_fusion
  18.2 3.0 fusion.19
  22.2 47.8 %all-gather.9.cloned.1.call-done = f32[2048,256]{1,0:T(8,128)} async-done(((f32[128,256]{1,0:T(8,128)}), f32[2048,256]{1,0:T(8,128)}) %all-gather.9.cloned.1.call-update) | async-done | bytes 2097168 | tf_op jit(solution)/shard_map/all_gather | solution.py:34
  70.0 1.8 reduce_sum.36
  72.5 3.9 gather_fusion.3
  76.5 3.9 gather_fusion.2
  83.8 41.4 %all-gather.11.cloned.1.call-done = f32[2048,256]{1,0:T(8,128)} async-done(((f32[128,256]{1,0:T(8,128)}), f32[2048,256]{1,0:T(8,128)}) %all-gather.11.cloned.1.call-update) | async-done | bytes 2097168 | tf_op jit(solution)/shard_map/all_gather | solution.py:34
  125.1 1.7 reduce_sum.37
  127.6 1.7 copy.15
  130.1 5.1 gather_fusion.5
  135.2 5.0 gather_fusion.4
  140.2 3.1 fusion.13
  145.2 41.4 %all-gather.13.cloned.1.call-done = f32[2048,256]{1,0:T(8,128)} async-done(((f32[128,256]{1,0:T(8,128)}), f32[2048,256]{1,0:T(8,128)}) %all-gather.13.cloned.1.call-update) | async-done | bytes 2097168 | tf_op jit(solution)/shard_map/all_gather | solution.py:34
  186.6 1.7 reduce_sum.38
  189.0 1.7 copy.16
  191.6 5.0 gather_fusion.7
  196.7 5.1 gather_fusion.6
  201.7 3.1 fusion.10
  206.7 41.4 %all-gather.15.cloned.1.call-done = f32[2048,256]{1,0:T(8,128)} async-done(((f32[128,256]{1,0:T(8,128)}), f32[2048,256]{1,0:T(8,128)}) %all-gather.15.cloned.1.call-update) | async-done | bytes 2097168 | tf_op jit(solution)/shard_map/all_gather | solution.py:34
  248.1 2.4 reduce_sum.39
  250.5 1.9 add_subtract_fusion
  254.8 1.6 fusion.7
  256.5 111.8 %all-reduce.9.cloned.1.call-done = f32[128,256]{1,0:T(8,128)} async-done(((f32[128,256]{1,0:T(8,128)}), f32[128,256]{1,0:T(8,128)}) %all-reduce.9.cloned.1.call-update) | async-done | bytes 131088 | tf_op jit(solution)/shard_map/psum | solution.py:53
  371.7 1.7 fusion.8
  373.6 113.3 %all-reduce.11.cloned.1.call-done = f32[128,256]{1,0:T(8,128)} async-done(((f32[128,256]{1,0:T(8,128)}), f32[128,256]{1,0:T(8,128)}) %all-reduce.11.cloned.1.call-update) | async-done | bytes 131088 | tf_op jit(solution)/shard_map/psum | solution.py:53
  489.3 1.7 fusion.9
  491.0 113.5 %all-reduce.13.cloned.1.call-done = f32[128,256]{1,0:T(8,128)} async-done(((f32[128,256]{1,0:T(8,128)}), f32[128,256]{1,0:T(8,128)}) %all-reduce.13.cloned.1.call-update) | async-done | bytes 131088 | tf_op jit(solution)/shard_map/psum | solution.py:53
  605.9 1.5 convolution_add_fusion.2
  608.5 1.8 fusion
  610.9 163.6 %all-reduce.15.cloned.1.call-done = f32[2080,256]{1,0:T(8,128)} async-done(((f32[2080,256]{1,0:T(8,128)}), f32[2080,256]{1,0:T(8,128)}) %all-reduce.15.cloned.1.call-update) | async-done | bytes 2129936 | tf_op jit(solution)/shard_map/psum | solution.py:87
  774.5 3.0 multiply_convert_fusion
  (82 shorter events, 25.5 us)
Async XLA Ops:
  7.2 62.8 %all-gather.9.cloned.1.call-start = ((), (), s32[]{:S(2)}) async-start(), calls=%async_computation.4 | async-start | bytes 2228224 | tf_op jit(solution)/shard_map/all_gather | solution.py:34
  18.1 3.0 copy-start
  21.1 50.6 %copy-start.10 = (bf16[128,2080]{0,1:T(8,128)(2,1)}, bf16[128,2080]{0,1:T(8,128)(2,1)S(1)}, u32[]{:S(2)}) copy-start(bf16[128,2080]{0,1:T(8,128)(2,1)S(1)} %fusion.19) | copy-start | bytes 1597444
  22.2 102.9 %all-gather.11.cloned.1.call-start = ((), (), s32[]{:S(2)}) async-start(), calls=%async_computation.5 | async-start | bytes 2228224 | tf_op jit(solution)/shard_map/all_gather | solution.py:34
  70.0 1.8 copy-start.12
  71.8 0.6 copy-start.14
  81.8 0.8 copy-start.5
  83.7 102.9 %all-gather.13.cloned.1.call-start = ((), (), s32[]{:S(2)}) async-start(), calls=%async_computation.6 | async-start | bytes 2228224 | tf_op jit(solution)/shard_map/all_gather | solution.py:34
  126.9 0.7 copy-start.15
  143.3 0.8 copy-start.6
  145.2 102.9 %all-gather.15.cloned.1.call-start = ((), (), s32[]{:S(2)}) async-start(), calls=%async_computation.7 | async-start | bytes 2228224 | tf_op jit(solution)/shard_map/all_gather | solution.py:34
  188.3 0.7 copy-start.16
  204.8 0.8 copy-start.8
  206.7 161.6 %all-reduce.9.cloned.1.call-start = ((), (), s32[]{:S(2)}) async-start(), calls=%async_computation | async-start | bytes 262144 | tf_op jit(solution)/shard_map/psum | solution.py:53
  252.3 1.2 copy-start.4
  253.6 1.2 copy-start.3
  256.5 230.5 %all-reduce.11.cloned.1.call-start = ((), (), s32[]{:S(2)}) async-start(), calls=%async_computation.1 | async-start | bytes 262144 | tf_op jit(solution)/shard_map/psum | solution.py:53
  369.2 1.2 copy-start.2
  370.4 1.2 copy-start.1
  373.3 231.2 %all-reduce.13.cloned.1.call-start = ((), (), s32[]{:S(2)}) async-start(), calls=%async_computation.2 | async-start | bytes 262144 | tf_op jit(solution)/shard_map/psum | solution.py:53
  489.3 115.3 %copy-start.11 = (bf16[128,2080]{0,1:T(8,128)(2,1)S(1)}, bf16[128,2080]{0,1:T(8,128)(2,1)}, u32[]{:S(2)}) copy-start(bf16[128,2080]{0,1:T(8,128)(2,1)} %copy-done.10) | copy-start | bytes 1597444
  491.0 283.5 %all-reduce.15.cloned.1.call-start = ((), (), s32[]{:S(2)}) async-start(), calls=%async_computation.3 | async-start | bytes 4259840 | tf_op jit(solution)/shard_map/psum | solution.py:87
  605.9 1.5 copy-start.7
  607.4 1.0 copy-start.9
  608.5 1.8 copy-start.17
  610.2 164.3 %copy-start.13 = (s32[2080,256]{1,0:T(8,128)S(1)}, s32[2080,256]{1,0:T(8,128)}, u32[]{:S(2)}) copy-start(s32[2080,256]{1,0:T(8,128)} %param.11) | copy-start | bytes 6389764
Sparse Core Ops, SparseCore 0:
  22.3 47.6 all-gather.8
  83.8 41.2 all-gather.10
  145.3 41.2 all-gather.12
  206.8 41.2 all-gather.14
  256.6 111.6 all-reduce.8
  373.5 113.4 all-reduce.10
  491.1 113.4 all-reduce.12
  610.4 164.1 all-reduce.14
